TPU v7x, 512 devices: a whole 4x8x8 slice. The times are simulated.
512 devices in a mesh: row: 16 (over y, core), col: 32 (over x, z).
Axes of the slice: x: 4, y: 8, z: 8, core: 2. Of those that a mesh axis runs over, the one named last changes fastest.
Arguments:
- hidden_acts: bfloat16 [256, 29568], P('row', 'col'), may hold values from -6 to 6
- output_errors: bfloat16 [256, 4096], P('col', 'row'), may hold values from -6 to 6
- col_points: int32 [32], replicated, may hold values from 0 to 64, as said below
- row_points: int32 [16], replicated, may hold values from 0 to 32, as said below
- worker_mask: int32 [16, 32], replicated, may hold values from 0 to 1, as said below
Outputs:
- clipped_grad: float32 [8, 512, 29568], P(None, 'col', 'row')
Inputs may be any that keep to these rules, and one draw needn't show every extreme that they name: `col_points`: distinct node indices. `row_points`: distinct node indices. `worker_mask`: each row of the grid has between 1 and 8 erased workers.
All inputs are finite; a program needn't handle non-finite values.
Results may differ from a plain program's by a relative error of at most 0.02.
Values may be sent and summed in bfloat16 or wider, within the bound.
No kernel may reach another device: no remote copies, remote signals or barrier semaphores. Data moves between devices by JAX's collectives and lax.ppermute only.
A program may use at most 128 MiB of HBM per device.

v0:
```python
import jax
import jax.numpy as jnp
from jax import lax
from jax.sharding import Mesh
from jax.sharding import PartitionSpec as P

D = 4096
FF = 29568
COL = ("col_0", "col_1")
ROW = ("row_0", "row_1")
ROW_COL = ("row_0", "row_1", "col_0", "col_1")


def copy_for_each(shard, axis):
    peers = lax.axis_size(axis)
    return lax.all_to_all(
        jnp.broadcast_to(shard[None], (peers, *shard.shape)), axis, 0, 0, tiled=True
    )


def laid_out(blocks, dim):
    lengths = list(blocks.shape[1:])
    lengths[dim] *= blocks.shape[0]
    return jnp.moveaxis(blocks, 0, dim).reshape(lengths)


def gathered_copies(shard, axis, dim):
    blocks = copy_for_each(shard, axis)
    return laid_out(blocks, dim)


def one_axis_at_a_time(shard, axes):
    for axis in axes:
        shard = lax.psum(shard, axis)
    return shard


def node_value(index, count):
    return jnp.cos(jnp.pi * (2.0 * index.astype(jnp.float32) + 1.0) / (2.0 * count))


def berrut(nodes, signs, live, targets):
    terms = (live * signs)[:, None] / (targets[None, :] - nodes[:, None])
    return terms / jnp.sum(terms, axis=0, keepdims=True)


def rank_signs(points, live):
    lower = (points[None, :] < points[:, None]).astype(jnp.int32)
    ranks = jnp.sum(lower * live[None, :], axis=1)
    return (1 - 2 * (ranks % 2)).astype(jnp.float32)


def encode_blocks(source, weights, block_count, block_width):

    def add_block(index, total):
        piece = lax.dynamic_slice_in_dim(source, index * block_width, block_width, 1).astype(
            jnp.float32
        )
        factor = lax.dynamic_slice_in_dim(weights, index, 1, 0)
        return total + factor * piece

    start = jnp.zeros((source.shape[0], block_width), jnp.float32)
    return lax.fori_loop(0, block_count, add_block, start).astype(jnp.bfloat16)


def shards(hidden_acts, output_errors, col_points, row_points, worker_mask):
    col_count = lax.axis_size(COL)
    row_count = lax.axis_size(ROW)
    col_place = lax.axis_index(COL)
    row_place = lax.axis_index(ROW)
    act_blocks = col_count // 2
    err_blocks = row_count // 2
    act_width = FF // act_blocks
    err_width = D // err_blocks
    data_acts = node_value(jnp.arange(act_blocks), act_blocks)
    data_errs = node_value(jnp.arange(err_blocks), err_blocks)
    work_acts = node_value(col_points, 2 * col_count + 1)
    work_errs = node_value(row_points, 2 * row_count + 1)
    alt_acts = (1 - 2 * (jnp.arange(act_blocks) % 2)).astype(jnp.float32)
    alt_errs = (1 - 2 * (jnp.arange(err_blocks) % 2)).astype(jnp.float32)
    full_acts = gathered_copies(hidden_acts, COL, 1)
    own_node = lax.dynamic_slice_in_dim(work_acts, col_place, 1, 0)
    encode_own = berrut(data_acts, alt_acts, jnp.ones((act_blocks,), jnp.float32), own_node)[:, 0]
    coded_acts = encode_blocks(full_acts, encode_own, act_blocks, act_width)
    full_errs = lax.all_gather(output_errors, ROW, axis=1, tiled=True)
    own_err = lax.dynamic_slice_in_dim(work_errs, row_place, 1, 0)
    encode_err = berrut(data_errs, alt_errs, jnp.ones((err_blocks,), jnp.float32), own_err)[:, 0]
    coded_errs = encode_blocks(full_errs, encode_err, err_blocks, err_width)
    all_errs = gathered_copies(coded_errs, COL, 0)
    product = lax.dot_general(
        all_errs,
        lax.all_gather(coded_acts, ROW, axis=0, tiled=True),
        (((0,), (0,)), ((), ())),
        preferred_element_type=jnp.float32,
    ).astype(jnp.bfloat16)
    live = lax.dynamic_slice_in_dim(worker_mask, row_place, 1, 0)[0]
    decode_acts = berrut(
        work_acts, rank_signs(col_points, live), live.astype(jnp.float32), data_acts
    )
    decoded = jnp.einsum(
        "jk,jrf->rkf",
        decode_acts,
        lax.all_to_all(product[None], COL, split_axis=1, concat_axis=0, tiled=True).astype(
            jnp.float32
        ),
    ).astype(jnp.bfloat16)
    decoded = decoded.reshape(decoded.shape[0], FF)
    all_rows = jnp.ones((row_count,), jnp.int32)
    decode_errs = berrut(
        work_errs, rank_signs(row_points, all_rows), jnp.ones((row_count,), jnp.float32), data_errs
    )
    grad = jnp.einsum(
        "il,irf->lrf",
        decode_errs,
        lax.all_to_all(decoded[None], ROW, split_axis=2, concat_axis=0, tiled=True).astype(
            jnp.float32
        ),
    )
    squares = one_axis_at_a_time(jnp.sum(grad * grad), ROW_COL)
    factor = jnp.minimum(1.0, jnp.sqrt(jnp.float32(FF * D)) / jnp.sqrt(squares + 1e-06))
    return grad * factor


def solution(mesh):
    finer = Mesh(mesh.devices.reshape(8, 2, 4, 8), ("row_0", "row_1", "col_0", "col_1"))
    in_specs = (P(ROW, COL), P(COL, ROW), P(), P(), P())
    out_specs = P(None, COL, ROW)
    return jax.shard_map(
        shards, mesh=finer, in_specs=in_specs, out_specs=out_specs, check_vma=False
    )
```

profile of v0, /device:TPU:8, one launch (start us, length us, event | category | flops | bytes accessed | tf_op | source)
XLA Modules:
  0.0 509.3 jit_solution(16859528297942924830)
XLA Ops:
  0.0 1.9 broadcast_in_dim.19
  1.9 13.2 %all-to-all-start.1 = ((bf16[32,16,924]{2,1,0:T(8,128)(2,1)}), bf16[32,16,924]{2,1,0:T(8,128)(2,1)S(1)}, u32[]{:S(2)}, u32[]{:S(2)}) async-start(bf16[32,16,924]{2,1,0:T(8,128)(2,1)} %broadcast_in_dim.19), calls=%async_computation.1 | async-start | bytes 2097152 | tf_op jit(solution)/shard_map/all_to_all | solution.py:16
  15.8 1.2 divide_reduce_fusion.1
  17.0 1.2 multiply_divide_fusion.1
  18.3 16.3 %all_gather.6 = bf16[8,4096]{1,0:T(8,128)(2,1)S(1)} all-gather(bf16[8,256]{1,0:T(8,128)(2,1)S(1)} %copy-done.1), channel_id=1, replica_groups=mesh['row_0'=8,'row_1'=2,'col_0'=4,'col_1'=8] {'row_0','row_1'}, dimensions={1}, use_global_device_ids=true | all-gather | bytes 69632 | tf_op jit(solution)/shard_map/all_gather | solution.py:85
  34.6 9.4 %while.28 = (s32[]{:T(128)}, f32[8,512]{1,0:T(8,128)S(1)}, f32[8]{0:T(128)S(1)}, bf16[8,4096]{1,0:T(8,128)(2,1)S(1)}, s32[]{:T(128)}, /*index=5*/s32[]{:T(128)}, s32[]{:T(128)}, s32[]{:T(128)}) while((s32[]{:T(128)}, f32[8,512]{1,0:T(8,128)S(1)}, f32[8]{0:T(128)S(1)}, bf16[8,4096]{1,0:T(8,128)(2,1)S(1)}, s32[]{:T(128)}, ...), condition=%wide.region_4.5_spmd.clone, body=%wide.region_3.4_spmd.clone.sunk | while | flops 16391 | bytes 41121 | solution.py:63
  46.2 1.3 divide_reduce_fusion
  47.5 1.3 multiply_divide_fusion
  49.5 9.8 %all-to-all-start = ((bf16[32,8,512]{2,1,0:T(8,128)(2,1)}), bf16[32,8,512]{2,1,0:T(8,128)(2,1)S(1)}, u32[]{:S(2)}, u32[]{:S(2)}) async-start(bf16[32,8,512]{2,1,0:T(8,128)(2,1)} %broadcast_in_dim.16), calls=%async_computation | async-start | bytes 524288 | tf_op jit(solution)/shard_map/all_to_all | solution.py:16
  59.9 1.3 reshape.108
  61.1 23.7 %while.29 = (s32[]{:T(128)}, f32[16,1848]{1,0:T(8,128)S(1)}, f32[16]{0:T(128)S(1)}, bf16[16,29568]{1,0:T(8,128)(2,1)S(1)}, s32[]{:T(128)}, /*index=5*/s32[]{:T(128)}, s32[]{:T(128)}, s32[]{:T(128)}) while((s32[]{:T(128)}, f32[16,1848]{1,0:T(8,128)S(1)}, f32[16]{0:T(128)S(1)}, bf16[16,29568]{1,0:T(8,128)(2,1)S(1)}, s32[]{:T(128)}, ...), condition=%wide.region_7.8_spmd.clone, body=%wide.region_6.7_spmd.clone.sunk | while | flops 118279 | bytes 295841 | solution.py:63
  61.8 0.8 select_add_fusion.5
  63.3 0.8 select_add_fusion.5
  64.8 0.8 select_add_fusion.5
  66.3 0.8 select_add_fusion.5
  67.8 0.8 select_add_fusion.5
  70.7 0.8 select_add_fusion.5
  72.2 0.8 select_add_fusion.5
  75.2 0.8 select_add_fusion.5
  76.6 0.8 select_add_fusion.5
  78.1 0.8 select_add_fusion.5
  79.6 0.8 select_add_fusion.5
  81.1 0.8 select_add_fusion.5
  82.6 0.8 select_add_fusion.5
  84.0 0.8 select_add_fusion.5
  84.9 18.8 %all_gather.7 = bf16[256,1848]{1,0:T(8,128)(2,1)S(1)} all-gather(bf16[16,1848]{1,0:T(8,128)(2,1)S(1)} %convert_element_type.115), channel_id=1, replica_groups=mesh['row_0'=8,'row_1'=2,'col_0'=4,'col_1'=8] {'row_0','row_1'}, dimensions={0}, use_global_device_ids=true | all-gather | bytes 1005312 | tf_op jit(solution)/shard_map/all_gather | solution.py:92
  104.4 6.8 %copy.23 = bf16[1,512,1848]{2,0,1:T(2,128)(2,1)} copy(bf16[1,512,1848]{1,2,0:T(8,128)(2,1)S(1)} %fusion) | data formatting | bytes 3784704 | tf_op jit(solution)/shard_map/broadcast_in_dim | solution.py:103
  111.7 12.9 %reduce.2 = bf16[512,1848]{1,0:T(8,128)(2,1)S(1)} reduce(bf16[512,1,1848]{2,1,0:T(2,128)(2,1)} %bitcast.43, bf16[]{:T(256)} %broadcast.315), dimensions={1}, to_apply=%bitcast.26.reduce_sub_computation | reduce | bytes 3784706
  124.6 4.5 reshape.111
  129.1 10.0 %all-to-all-start.2 = ((bf16[32,2,14784]{2,1,0:T(2,128)(2,1)}), bf16[32,2,14784]{2,1,0:T(2,128)(2,1)S(1)}, u32[]{:S(2)}, u32[]{:S(2)}) async-start(bf16[32,2,14784]{2,1,0:T(2,128)(2,1)} %reshape.111), calls=%async_computation.2 | async-start | bytes 3801088 | tf_op jit(solution)/shard_map/all_to_all | solution.py:103
  139.3 46.1 %all-to-all-done.2 = bf16[32,2,14784]{2,1,0:T(2,128)(2,1)S(1)} async-done(((bf16[32,2,14784]{2,1,0:T(2,128)(2,1)}), bf16[32,2,14784]{2,1,0:T(2,128)(2,1)S(1)}, u32[]{:S(2)}, u32[]{:S(2)}) %all-to-all-start.2) | async-done | bytes 1892384 | tf_op jit(solution)/shard_map/all_to_all | solution.py:103
  185.4 7.4 %reshape.112 = bf16[512,1,1848]{2,1,0:T(2,128)(2,1)} reshape(bf16[32,2,14784]{2,1,0:T(2,128)(2,1)S(1)} %all-to-all-done.2) | data formatting | bytes 3784704
  192.8 2.4 copy.28
  195.7 1.0 broadcast_in_dim_reshape.3
  196.7 22.8 %copy.25 = bf16[1,16,29568]{1,0,2:T(2,128)(2,1)} copy(bf16[1,16,29568]{2,1,0:T(8,128)(2,1)S(1)} %broadcast_in_dim_reshape.3) | data formatting | bytes 1892352 | tf_op jit(solution)/shard_map/broadcast_in_dim;reshape | solution.py:115
  219.5 162.1 %reduce.3 = bf16[29568,16]{1,0:T(8,128)(2,1)} reduce(bf16[29568,1,16]{2,1,0:T(2,128)(2,1)} %bitcast.41, bf16[]{:T(256)} %broadcast.315), dimensions={1}, to_apply=%bitcast.28.reduce_sub_computation | reduce | bytes 1892354
  381.6 10.5 %reshape.113 = bf16[16,2,14784]{2,1,0:T(2,128)(2,1)} reshape(bf16[29568,16]{1,0:T(8,128)(2,1)} %reduce.3) | data formatting | bytes 1892352
  392.1 5.5 %all-to-all-start.3 = ((bf16[16,2,14784]{2,1,0:T(2,128)(2,1)}), bf16[16,2,14784]{2,1,0:T(2,128)(2,1)S(1)}, u32[]{:S(2)}, u32[]{:S(2)}) async-start(bf16[16,2,14784]{2,1,0:T(2,128)(2,1)} %reshape.113), calls=%async_computation.3 | async-start | bytes 1900544 | tf_op jit(solution)/shard_map/all_to_all | solution.py:115
  398.1 22.2 %all-to-all-done.3 = bf16[16,2,14784]{2,1,0:T(2,128)(2,1)S(1)} async-done(((bf16[16,2,14784]{2,1,0:T(2,128)(2,1)}), bf16[16,2,14784]{2,1,0:T(2,128)(2,1)S(1)}, u32[]{:S(2)}, u32[]{:S(2)}) %all-to-all-start.3) | async-done | bytes 946208 | tf_op jit(solution)/shard_map/all_to_all | solution.py:115
  420.3 11.2 %reshape.114 = bf16[29568,1,16]{2,1,0:T(2,128)(2,1)} reshape(bf16[16,2,14784]{2,1,0:T(2,128)(2,1)S(1)} %all-to-all-done.3) | data formatting | bytes 1892352
  431.5 27.1 %copy.26 = bf16[1,16,29568]{2,1,0:T(8,128)(2,1)S(1)} copy(bf16[1,16,29568]{1,0,2:T(2,128)(2,1)} %bitcast.42) | data formatting | bytes 1892352 | tf_op jit(solution)/shard_map/all_to_all | solution.py:115
  458.6 1.6 all_to_all.33
  460.2 1.1 multiply_reduce_fusion
  461.3 16.6 %psum.28 = f32[]{:T(128)} all-reduce(f32[]{:T(128)} %get-tuple-element.211), channel_id=1, replica_groups=mesh['row_0'=8,'row_1'=2,'col_0'=4,'col_1'=8] {'row_0'}, use_global_device_ids=true, to_apply=%region_11.12 | all-reduce | flops 1 | bytes 8 | tf_op jit(solution)/shard_map/psum | solution.py:34
  477.9 3.1 psum.29
  481.0 9.2 %psum.30 = f32[]{:T(128)} all-reduce(f32[]{:T(128)} %psum.29), channel_id=1, replica_groups=mesh['row_0'=8,'row_1'=2,'col_0'=4,'col_1'=8] {'col_0'}, use_global_device_ids=true, to_apply=%region_13.14 | all-reduce | flops 1 | bytes 8 | tf_op jit(solution)/shard_map/psum | solution.py:34
  490.1 17.3 %psum.31 = f32[]{:T(128)} all-reduce(f32[]{:T(128)} %psum.30), channel_id=1, replica_groups=mesh['row_0'=8,'row_1'=2,'col_0'=4,'col_1'=8] {'col_1'}, use_global_device_ids=true, to_apply=%region_14.15 | all-reduce | flops 1 | bytes 8 | tf_op jit(solution)/shard_map/psum | solution.py:34
  508.2 1.1 copy.27
  (64 shorter events, 28.1 us)
Async XLA Ops:
  0.0 15.1 %copy-start.2 = (s32[16]{0:T(128)S(1)}, s32[16]{0:T(128)}, u32[]{:S(2)}) copy-start(s32[16]{0:T(128)} %param.12) | copy-start | bytes 196
  0.0 18.2 %copy-start.1 = (bf16[8,256]{1,0:T(8,128)(2,1)S(1)}, bf16[8,256]{1,0:T(8,128)(2,1)}, u32[]{:S(2)}) copy-start(bf16[8,256]{1,0:T(8,128)(2,1)} %param.10) | copy-start | bytes 12292
  0.0 44.7 %copy-start = (s32[32]{0:T(128)S(1)}, s32[32]{0:T(128)}, u32[]{:S(2)}) copy-start(s32[32]{0:T(128)} %param.11) | copy-start | bytes 388
  1.9 46.9 %all-to-all-start.1 = ((bf16[32,16,924]{2,1,0:T(8,128)(2,1)}), bf16[32,16,924]{2,1,0:T(8,128)(2,1)S(1)}, u32[]{:S(2)}, u32[]{:S(2)}) async-start(bf16[32,16,924]{2,1,0:T(8,128)(2,1)} %broadcast_in_dim.19), calls=%async_computation.1 | async-start | bytes 2097152 | tf_op jit(solution)/shard_map/all_to_all | solution.py:16
  49.5 54.2 %all-to-all-start = ((bf16[32,8,512]{2,1,0:T(8,128)(2,1)}), bf16[32,8,512]{2,1,0:T(8,128)(2,1)S(1)}, u32[]{:S(2)}, u32[]{:S(2)}) async-start(bf16[32,8,512]{2,1,0:T(8,128)(2,1)} %broadcast_in_dim.16), calls=%async_computation | async-start | bytes 524288 | tf_op jit(solution)/shard_map/all_to_all | solution.py:16
  129.1 56.3 %all-to-all-start.2 = ((bf16[32,2,14784]{2,1,0:T(2,128)(2,1)}), bf16[32,2,14784]{2,1,0:T(2,128)(2,1)S(1)}, u32[]{:S(2)}, u32[]{:S(2)}) async-start(bf16[32,2,14784]{2,1,0:T(2,128)(2,1)} %reshape.111), calls=%async_computation.2 | async-start | bytes 3801088 | tf_op jit(solution)/shard_map/all_to_all | solution.py:103
  392.1 28.2 %all-to-all-start.3 = ((bf16[16,2,14784]{2,1,0:T(2,128)(2,1)}), bf16[16,2,14784]{2,1,0:T(2,128)(2,1)S(1)}, u32[]{:S(2)}, u32[]{:S(2)}) async-start(bf16[16,2,14784]{2,1,0:T(2,128)(2,1)} %reshape.113), calls=%async_computation.3 | async-start | bytes 1900544 | tf_op jit(solution)/shard_map/all_to_all | solution.py:115
where the time goes:
time: 511 us; the launch traced here: 509 us
  other arithmetic  199 us (39%)
  local copies, waits for them, and re-layouts  118 us (23%)
  blocking collectives  81.3 us (16%)
  waiting for transfers between devices  68.3 us (13%)
  starting transfers between devices  38.5 us (8%)
    unnamed x4, other arithmetic  175 us
    psum x4, blocking collectives, one_axis_at_a_time(): shard = lax.psum(shard, axis)  46.1 us
    all_to_all x1, waiting for transfers between devices, shards(): lax.all_to_all(product[None], COL, split_axis=1, concat_axis=0, tiled=True)  46.1 us
    unnamed x12, local copies, waits for them, and re-layouts  36.5 us
    all_to_all x2, local copies, waits for them, and re-layouts, shards(): lax.all_to_all(decoded[None], ROW, split_axis=2, concat_axis=0, tiled=True)  28.6 us
    another operation x2, local copies, waits for them, and re-layouts, shards(): decoded[None]  23.8 us
    all_to_all x2, starting transfers between devices, copy_for_each(): lax.all_to_all(jnp.broadcast_to(shard[None], (peers, *shard.shape)), axis...  22.9 us
    all_to_all x1, waiting for transfers between devices, shards(): lax.all_to_all(decoded[None], ROW, split_axis=2, concat_axis=0, tiled=True)  22.2 us
  transfers between devices with their start and end apart: 4, of which 2 were waited for; matrix products, arithmetic and copies ran while one was open for 8% of the time, Pallas kernels for 0%

commit v1 on v0

--- a/solution.py
+++ b/solution.py
@@ -112,9 +112,12 @@
     grad = jnp.einsum(
         "il,irf->lrf",
         decode_errs,
-        lax.all_to_all(decoded[None], ROW, split_axis=2, concat_axis=0, tiled=True).astype(
-            jnp.float32
-        ),
+        jnp.concatenate(
+            lax.all_to_all(
+                jnp.stack(jnp.split(decoded[None], lax.axis_size(ROW), axis=2)), ROW, 0, 0
+            ),
+            axis=0,
+        ).astype(jnp.float32),
     )
     squares = one_axis_at_a_time(jnp.sum(grad * grad), ROW_COL)
     factor = jnp.minimum(1.0, jnp.sqrt(jnp.float32(FF * D)) / jnp.sqrt(squares + 1e-06))

time: 511 us -> 287 us (0.56)
  other arithmetic: 199 us -> 36.8 us
  local copies, waits for them, and re-layouts: 118 us -> 56.7 us
    unnamed x4 -> x3, other arithmetic: 175 us -> 12.9 us
    all_to_all x2 -> x0, local copies, waits for them, and re-layouts: 28.6 us -> none  [shards(): lax.all_to_all(decoded[None], ROW, split_axis=2, concat_axis=0, tiled=True)]
    another operation x2 -> x1, local copies, waits for them, and re-layouts: 23.8 us -> 1 us  [shards(): decoded[None]]
    unnamed x12 -> x25, local copies, waits for them, and re-layouts: 36.5 us -> 25.4 us
  transfers between devices with their start and end apart: 4 -> 4, of which waited for: 2 -> 2; matrix products, arithmetic and copies ran while one was open for 8% -> 15% of each run, Pallas kernels for 0% -> 0%
where the time goes in v1:
time: 287 us; the launch traced here: 286 us
  blocking collectives  81.4 us (28%)
  waiting for transfers between devices  69.2 us (24%)
  local copies, waits for them, and re-layouts  56.7 us (20%)
  starting transfers between devices  38.3 us (13%)
  other arithmetic  36.8 us (13%)
    all_to_all x1, waiting for transfers between devices, shards(): lax.all_to_all(product[None], COL, split_axis=1, concat_axis=0, tiled=True)  46.3 us
    psum x4, blocking collectives, one_axis_at_a_time(): shard = lax.psum(shard, axis)  46.3 us
    unnamed x25, local copies, waits for them, and re-layouts  25.4 us
    all_to_all x2, starting transfers between devices, copy_for_each(): lax.all_to_all(jnp.broadcast_to(shard[None], (peers, *shard.shape)), axis...  22.9 us
    all_to_all x1, waiting for transfers between devices, shards(): lax.all_to_all(jnp.stack(jnp.split(decoded[None], lax.axis_size(ROW), axi...  22.9 us
    all_gather x1, blocking collectives, shards(): lax.all_gather(coded_acts, ROW, axis=0, tiled=True)  18.8 us
    add x24, other arithmetic, add_block(): return total + factor * piece  17.1 us
    all_gather x1, blocking collectives, shards(): full_errs = lax.all_gather(output_errors, ROW, axis=1, tiled=True)  16.3 us
  transfers between devices with their start and end apart: 4, of which 2 were waited for; matrix products, arithmetic and copies ran while one was open for 15% of the time, Pallas kernels for 0%

profile of v1, /device:TPU:8, one launch (start us, length us, event | category | flops | bytes accessed | tf_op | source)
XLA Modules:
  0.0 286.2 jit_solution(11174596957337147805)
XLA Ops:
  0.0 1.9 broadcast_in_dim.19
  1.9 13.2 %all-to-all-start.1 = ((bf16[32,16,924]{2,1,0:T(8,128)(2,1)}), bf16[32,16,924]{2,1,0:T(8,128)(2,1)S(1)}, u32[]{:S(2)}, u32[]{:S(2)}) async-start(bf16[32,16,924]{2,1,0:T(8,128)(2,1)} %broadcast_in_dim.19), calls=%async_computation.1 | async-start | bytes 2097152 | tf_op jit(solution)/shard_map/all_to_all | solution.py:16
  15.8 1.2 divide_reduce_fusion.1
  17.0 1.2 multiply_divide_fusion.1
  18.3 16.3 %all_gather.6 = bf16[8,4096]{1,0:T(8,128)(2,1)S(1)} all-gather(bf16[8,256]{1,0:T(8,128)(2,1)S(1)} %copy-done.1), channel_id=1, replica_groups=mesh['row_0'=8,'row_1'=2,'col_0'=4,'col_1'=8] {'row_0','row_1'}, dimensions={1}, use_global_device_ids=true | all-gather | bytes 69632 | tf_op jit(solution)/shard_map/all_gather | solution.py:85
  34.6 9.4 %while.28 = (s32[]{:T(128)}, f32[8,512]{1,0:T(8,128)S(1)}, f32[8]{0:T(128)S(1)}, bf16[8,4096]{1,0:T(8,128)(2,1)S(1)}, s32[]{:T(128)}, /*index=5*/s32[]{:T(128)}, s32[]{:T(128)}, s32[]{:T(128)}) while((s32[]{:T(128)}, f32[8,512]{1,0:T(8,128)S(1)}, f32[8]{0:T(128)S(1)}, bf16[8,4096]{1,0:T(8,128)(2,1)S(1)}, s32[]{:T(128)}, ...), condition=%wide.region_4.5_spmd.clone, body=%wide.region_3.4_spmd.clone.sunk | while | flops 16391 | bytes 41121 | solution.py:63
  44.9 0.7 fusion.51
  46.2 1.3 divide_reduce_fusion
  47.5 1.3 multiply_divide_fusion
  48.8 0.7 broadcast_in_dim.16
  49.5 9.8 %all-to-all-start = ((bf16[32,8,512]{2,1,0:T(8,128)(2,1)}), bf16[32,8,512]{2,1,0:T(8,128)(2,1)S(1)}, u32[]{:S(2)}, u32[]{:S(2)}) async-start(bf16[32,8,512]{2,1,0:T(8,128)(2,1)} %broadcast_in_dim.16), calls=%async_computation | async-start | bytes 524288 | tf_op jit(solution)/shard_map/all_to_all | solution.py:16
  59.9 1.3 reshape.111
  61.1 23.7 %while.29 = (s32[]{:T(128)}, f32[16,1848]{1,0:T(8,128)S(1)}, f32[16]{0:T(128)S(1)}, bf16[16,29568]{1,0:T(8,128)(2,1)S(1)}, s32[]{:T(128)}, /*index=5*/s32[]{:T(128)}, s32[]{:T(128)}, s32[]{:T(128)}) while((s32[]{:T(128)}, f32[16,1848]{1,0:T(8,128)S(1)}, f32[16]{0:T(128)S(1)}, bf16[16,29568]{1,0:T(8,128)(2,1)S(1)}, s32[]{:T(128)}, ...), condition=%wide.region_7.8_spmd.clone, body=%wide.region_6.7_spmd.clone.sunk | while | flops 118279 | bytes 295841 | solution.py:63
  61.8 0.8 select_add_fusion.5
  63.3 0.8 select_add_fusion.5
  64.8 0.8 select_add_fusion.5
  66.3 0.8 select_add_fusion.5
  67.8 0.8 select_add_fusion.5
  69.2 0.8 select_add_fusion.5
  70.7 0.8 select_add_fusion.5
  72.2 0.8 select_add_fusion.5
  73.7 0.8 select_add_fusion.5
  75.2 0.8 select_add_fusion.5
  76.6 0.8 select_add_fusion.5
  78.1 0.8 select_add_fusion.5
  79.6 0.8 select_add_fusion.5
  81.1 0.8 select_add_fusion.5
  82.6 0.8 select_add_fusion.5
  84.0 0.8 select_add_fusion.5
  84.9 18.8 %all_gather.7 = bf16[256,1848]{1,0:T(8,128)(2,1)S(1)} all-gather(bf16[16,1848]{1,0:T(8,128)(2,1)S(1)} %convert_element_type.115), channel_id=1, replica_groups=mesh['row_0'=8,'row_1'=2,'col_0'=4,'col_1'=8] {'row_0','row_1'}, dimensions={0}, use_global_device_ids=true | all-gather | bytes 1005312 | tf_op jit(solution)/shard_map/all_gather | solution.py:92
  104.4 6.8 %copy.322 = bf16[1,512,1848]{2,0,1:T(2,128)(2,1)} copy(bf16[1,512,1848]{1,2,0:T(8,128)(2,1)S(1)} %fusion) | data formatting | bytes 3784704 | tf_op jit(solution)/shard_map/broadcast_in_dim | solution.py:103
  111.7 12.9 %reduce.2 = bf16[512,1848]{1,0:T(8,128)(2,1)S(1)} reduce(bf16[512,1,1848]{2,1,0:T(2,128)(2,1)} %bitcast.101, bf16[]{:T(256)} %broadcast.315), dimensions={1}, to_apply=%bitcast.88.reduce_sub_computation | reduce | bytes 3784706
  124.6 4.5 %reshape.115 = bf16[32,2,14784]{2,1,0:T(2,128)(2,1)} reshape(bf16[512,1848]{1,0:T(8,128)(2,1)S(1)} %reduce.2) | data formatting | bytes 3784704
  129.1 9.8 %all-to-all-start.2 = ((bf16[32,2,14784]{2,1,0:T(2,128)(2,1)}), bf16[32,2,14784]{2,1,0:T(2,128)(2,1)S(1)}, u32[]{:S(2)}, u32[]{:S(2)}) async-start(bf16[32,2,14784]{2,1,0:T(2,128)(2,1)} %reshape.115), calls=%async_computation.2 | async-start | bytes 3801088 | tf_op jit(solution)/shard_map/all_to_all | solution.py:103
  139.1 46.3 %all-to-all-done.2 = bf16[32,2,14784]{2,1,0:T(2,128)(2,1)S(1)} async-done(((bf16[32,2,14784]{2,1,0:T(2,128)(2,1)}), bf16[32,2,14784]{2,1,0:T(2,128)(2,1)S(1)}, u32[]{:S(2)}, u32[]{:S(2)}) %all-to-all-start.2) | async-done | bytes 1892384 | tf_op jit(solution)/shard_map/all_to_all | solution.py:103
  185.4 7.4 %reshape.116 = bf16[512,1,1848]{2,1,0:T(2,128)(2,1)} reshape(bf16[32,2,14784]{2,1,0:T(2,128)(2,1)S(1)} %all-to-all-done.2) | data formatting | bytes 3784704
  192.8 2.4 copy.326
  195.7 1.0 broadcast_in_dim_reshape.3
  200.2 0.7 fusion.17
  200.9 0.7 fusion.16
  208.0 5.6 %all-to-all-start.3 = ((bf16[16,1,16,1848]{3,2,1,0:T(8,128)(2,1)}), bf16[16,1,16,1848]{3,2,1,0:T(8,128)(2,1)S(1)}, u32[]{:S(2)}, u32[]{:S(2)}) async-start(bf16[16,1,16,1848]{3,2,1,0:T(8,128)(2,1)} %fusion.7), calls=%async_computation.3 | async-start | bytes 1966080 | tf_op jit(solution)/shard_map/all_to_all | solution.py:116
  214.0 22.9 %all-to-all-done.3 = bf16[16,1,16,1848]{3,2,1,0:T(8,128)(2,1)S(1)} async-done(((bf16[16,1,16,1848]{3,2,1,0:T(8,128)(2,1)}), bf16[16,1,16,1848]{3,2,1,0:T(8,128)(2,1)S(1)}, u32[]{:S(2)}, u32[]{:S(2)}) %all-to-all-start.3) | async-done | bytes 946208 | tf_op jit(solution)/shard_map/all_to_all | solution.py:116
  236.9 1.1 multiply_reduce_fusion
  238.0 16.7 %psum.28 = f32[]{:T(128)} all-reduce(f32[]{:T(128)} %get-tuple-element.211), channel_id=1, replica_groups=mesh['row_0'=8,'row_1'=2,'col_0'=4,'col_1'=8] {'row_0'}, use_global_device_ids=true, to_apply=%region_11.12 | all-reduce | flops 1 | bytes 8 | tf_op jit(solution)/shard_map/psum | solution.py:34
  254.8 3.1 %psum.29 = f32[]{:T(128)} all-reduce(f32[]{:T(128)} %psum.28), channel_id=1, replica_groups=mesh['row_0'=8,'row_1'=2,'col_0'=4,'col_1'=8] {'row_1'}, use_global_device_ids=true, to_apply=%region_12.13 | all-reduce | flops 1 | bytes 8 | tf_op jit(solution)/shard_map/psum | solution.py:34
  257.8 9.1 %psum.30 = f32[]{:T(128)} all-reduce(f32[]{:T(128)} %psum.29), channel_id=1, replica_groups=mesh['row_0'=8,'row_1'=2,'col_0'=4,'col_1'=8] {'col_0'}, use_global_device_ids=true, to_apply=%region_13.14 | all-reduce | flops 1 | bytes 8 | tf_op jit(solution)/shard_map/psum | solution.py:34
  267.0 17.3 %psum.31 = f32[]{:T(128)} all-reduce(f32[]{:T(128)} %psum.30), channel_id=1, replica_groups=mesh['row_0'=8,'row_1'=2,'col_0'=4,'col_1'=8] {'col_1'}, use_global_device_ids=true, to_apply=%region_14.15 | all-reduce | flops 1 | bytes 8 | tf_op jit(solution)/shard_map/psum | solution.py:34
  285.1 1.1 copy.325
  (74 shorter events, 35.0 us)
Async XLA Ops:
  0.0 15.1 %copy-start.2 = (s32[16]{0:T(128)S(1)}, s32[16]{0:T(128)}, u32[]{:S(2)}) copy-start(s32[16]{0:T(128)} %param.12) | copy-start | bytes 196
  0.0 18.2 %copy-start.1 = (bf16[8,256]{1,0:T(8,128)(2,1)S(1)}, bf16[8,256]{1,0:T(8,128)(2,1)}, u32[]{:S(2)}) copy-start(bf16[8,256]{1,0:T(8,128)(2,1)} %param.10) | copy-start | bytes 12292
  0.0 44.7 %copy-start = (s32[32]{0:T(128)S(1)}, s32[32]{0:T(128)}, u32[]{:S(2)}) copy-start(s32[32]{0:T(128)} %param.11) | copy-start | bytes 388
  1.9 46.9 %all-to-all-start.1 = ((bf16[32,16,924]{2,1,0:T(8,128)(2,1)}), bf16[32,16,924]{2,1,0:T(8,128)(2,1)S(1)}, u32[]{:S(2)}, u32[]{:S(2)}) async-start(bf16[32,16,924]{2,1,0:T(8,128)(2,1)} %broadcast_in_dim.19), calls=%async_computation.1 | async-start | bytes 2097152 | tf_op jit(solution)/shard_map/all_to_all | solution.py:16
  49.5 54.2 %all-to-all-start = ((bf16[32,8,512]{2,1,0:T(8,128)(2,1)}), bf16[32,8,512]{2,1,0:T(8,128)(2,1)S(1)}, u32[]{:S(2)}, u32[]{:S(2)}) async-start(bf16[32,8,512]{2,1,0:T(8,128)(2,1)} %broadcast_in_dim.16), calls=%async_computation | async-start | bytes 524288 | tf_op jit(solution)/shard_map/all_to_all | solution.py:16
  129.1 56.3 %all-to-all-start.2 = ((bf16[32,2,14784]{2,1,0:T(2,128)(2,1)}), bf16[32,2,14784]{2,1,0:T(2,128)(2,1)S(1)}, u32[]{:S(2)}, u32[]{:S(2)}) async-start(bf16[32,2,14784]{2,1,0:T(2,128)(2,1)} %reshape.115), calls=%async_computation.2 | async-start | bytes 3801088 | tf_op jit(solution)/shard_map/all_to_all | solution.py:103
  208.0 28.9 %all-to-all-start.3 = ((bf16[16,1,16,1848]{3,2,1,0:T(8,128)(2,1)}), bf16[16,1,16,1848]{3,2,1,0:T(8,128)(2,1)S(1)}, u32[]{:S(2)}, u32[]{:S(2)}) async-start(bf16[16,1,16,1848]{3,2,1,0:T(8,128)(2,1)} %fusion.7), calls=%async_computation.3 | async-start | bytes 1966080 | tf_op jit(solution)/shard_map/all_to_all | solution.py:116
